TPU v7x, 256 devices: a whole 4x4x8 slice. The times are simulated.
256 devices in a mesh: seq: 32 (over x_lo, z, core), band: 8 (over y, x_hi).
Axes of the slice: x: 4 (x_hi: 2, x_lo: 2; x = x_hi * 2 + x_lo), y: 4, z: 8, core: 2. Of those that a mesh axis runs over, the one named last changes fastest.
Arguments:
- tokens: bfloat16 [4096, 1024], P('seq', 'band'), may hold values from -6 to 6
- mappable: int32 [4096], P('seq'), may hold values 0 or 1
- attn_gain: float32 [1024], replicated, may hold values from 0.1 to 1.9
- w_query: bfloat16 [1024, 1024], P(None, 'band'), may hold values from -1 to 1
- w_key: bfloat16 [1024, 1024], P(None, 'band'), may hold values from -4 to 4
- w_value: bfloat16 [1024, 1024], P(None, 'band'), may hold values from -0.1875 to 0.1875
- w_out: bfloat16 [1024, 1024], P('band'), may hold values from -0.75 to 0.75
- w_left: bfloat16 [1024, 128], replicated, may hold values from -0.1875 to 0.1875
- w_right: bfloat16 [1024, 128], replicated, may hold values from -0.1875 to 0.1875
- conv_gain: float32 [2, 128], replicated, may hold values from 0.1 to 1.9
- conv_kernel: bfloat16 [2, 3, 3, 128, 128], replicated, may hold values from -0.1875 to 0.1875
- conv_bias: float32 [2, 128], replicated, may hold values from -3 to 3
- contact_weight: float32 [128], replicated, may hold values from -0.5 to 0.5
Outputs:
- trunk_out: bfloat16 [4096, 1024], P('seq', 'band')
- contacts: float32 [4096, 256], P('seq', 'band')
All inputs are finite; a program needn't handle non-finite values. No bound on the sum of `mappable` on one device may be relied on, other than what follows from the above.
Results may differ from a plain program's by a relative error of at most 0.035.
Values may be sent and summed in bfloat16 or wider, within the bound.
A program may use at most 64 MiB of HBM per device.

v0:
```python
import jax
import jax.numpy as jnp
from jax import lax
from jax.sharding import PartitionSpec as P

HEAD = 128
CONVS = 2
DIAG = 32
epsilon = 1e-06


def passed_along(value, axis, steps):
    count = lax.axis_size(axis)
    initial, last = (max(0, -steps), min(count, count - steps))
    return lax.ppermute(value, axis, [(source, source + steps) for source in range(initial, last)])


def extended(x, sides, width):
    for axis, dim in sides:
        size, length = (lax.axis_size(axis), x.shape[dim])
        up = [(i, (i + 1) % size) for i in range(size - 1)]
        down = [(j, i) for i, j in up]
        last = lax.slice_in_dim(x, length - width, length, axis=dim)
        initial = lax.slice_in_dim(x, 0, width, axis=dim)
        before = lax.ppermute(last, axis, up)
        after = lax.ppermute(initial, axis, down)
        x = jnp.concatenate([before, x, after], axis=dim)
    return x


def rms_scale(values, gain):
    floats = values.astype(jnp.float32)
    return floats * lax.rsqrt(jnp.mean(floats * floats, axis=-1, keepdims=True) + epsilon) * gain


def shear_conv(padded, kernel, spread):
    out_rows = padded.shape[0] - 2 * spread
    out_diags = padded.shape[1] - 4 * spread
    windows = []
    for tap_row in range(3):
        for tap_col in range(3):
            row_first = spread * tap_row
            diag_first = 2 * spread + spread * (tap_col - tap_row)
            windows.append(
                padded[row_first : row_first + out_rows, diag_first : diag_first + out_diags]
            )
    stacked = jnp.concatenate(windows, axis=-1)
    flat_kernel = kernel.reshape(9 * kernel.shape[-2], kernel.shape[-1])
    return jnp.einsum("aek,kf->aef", stacked, flat_kernel, preferred_element_type=jnp.float32)


def valid_cells(row_first, diag_first, row_count, diag_count, length, band_width):
    rows_glob = row_first + jnp.arange(row_count, dtype=jnp.int32)
    diags_glob = diag_first + jnp.arange(diag_count, dtype=jnp.int32)
    inside = (
        (rows_glob[:, None] >= 0)
        & (rows_glob[:, None] < length)
        & (diags_glob[None, :] >= 0)
        & (diags_glob[None, :] < band_width)
        & (rows_glob[:, None] + diags_glob[None, :] < length)
    )
    return jnp.where(inside, 1.0, 0.0).astype(jnp.float32)[:, :, None]


def local(
    tokens,
    mappable,
    attn_gain,
    w_query,
    w_key,
    w_value,
    w_out,
    w_left,
    w_right,
    conv_gain,
    conv_kernel,
    conv_bias,
    contact_weight,
):
    row_count = tokens.shape[0]
    feature_share = tokens.shape[1]
    heads_here = w_query.shape[1] // HEAD
    seq_index = lax.axis_index("seq")
    band_index = lax.axis_index("band")
    length = row_count * lax.axis_size("seq")
    band_width = DIAG * lax.axis_size("band")
    gathered = lax.all_gather(tokens, "band", axis=1, tiled=True)
    normed = rms_scale(gathered, attn_gain).astype(jnp.bfloat16)
    query = jnp.dot(normed, w_query, preferred_element_type=jnp.float32).astype(jnp.bfloat16)
    key_rows = jnp.dot(normed, w_key, preferred_element_type=jnp.float32).astype(jnp.bfloat16)
    value = jnp.dot(normed, w_value, preferred_element_type=jnp.float32).astype(jnp.bfloat16)
    key_offset = ((mappable - 1).astype(jnp.float32) * 1000000000.0).astype(jnp.bfloat16)
    query_heads = query.reshape(row_count, heads_here, HEAD)
    row_top = jnp.full((heads_here, row_count), -jnp.inf, jnp.float32)
    weight_sum = jnp.zeros((heads_here, row_count), jnp.float32)
    mixed_sum = jnp.zeros((heads_here, row_count, HEAD), jnp.float32)
    key_piece = lax.all_gather(key_rows, "seq", axis=0, tiled=True)
    value_piece = lax.all_gather(value, "seq", axis=0, tiled=True)
    offset_piece = lax.all_gather(key_offset, "seq", axis=0, tiled=True)
    piece_rows = key_piece.shape[0]
    key_heads = key_piece.reshape(piece_rows, heads_here, HEAD)
    value_heads = value_piece.reshape(piece_rows, heads_here, HEAD)
    scores = (
        jnp.einsum("thd,nhd->htn", query_heads, key_heads, preferred_element_type=jnp.float32)
        * HEAD ** (-0.5)
        + offset_piece.astype(jnp.float32)[None, None, :]
    )
    new_top = jnp.max(scores, axis=2)
    weights = jnp.exp(scores - new_top[:, :, None])
    fade = jnp.exp(row_top - new_top)
    weight_sum = weight_sum * fade + jnp.sum(weights, axis=2)
    mixed_sum = mixed_sum * fade[:, :, None] + jnp.einsum(
        "htn,nhd->htd",
        weights.astype(jnp.bfloat16),
        value_heads,
        preferred_element_type=jnp.float32,
    )
    row_top, weight_sum, mixed_sum = (new_top, weight_sum, mixed_sum)
    attended = (
        (mixed_sum / weight_sum[:, :, None])
        .astype(jnp.bfloat16)
        .transpose(1, 0, 2)
        .reshape(row_count, heads_here * HEAD)
    )
    projected = jnp.dot(attended, w_out, preferred_element_type=jnp.float32)
    keep_rows = mappable.astype(jnp.bfloat16)[:, None]
    summed = lax.psum_scatter(
        projected.astype(jnp.bfloat16), "band", scatter_dimension=1, tiled=True
    ).astype(jnp.float32)
    trunk_out = (tokens.astype(jnp.float32) + summed).astype(jnp.bfloat16)
    rows_left = lax.dynamic_slice_in_dim(w_left, band_index * feature_share, feature_share, 0)
    rows_right = lax.dynamic_slice_in_dim(w_right, band_index * feature_share, feature_share, 0)
    part_left, part_right = (
        lax.psum(
            jnp.dot(trunk_out, rows_left, preferred_element_type=jnp.float32).astype(jnp.bfloat16),
            "band",
        ).astype(jnp.float32),
        lax.psum(
            jnp.dot(trunk_out, rows_right, preferred_element_type=jnp.float32).astype(jnp.bfloat16),
            "band",
        ).astype(jnp.float32),
    )
    left_side = part_left.astype(jnp.bfloat16) * keep_rows
    right_side = part_right.astype(jnp.bfloat16) * keep_rows
    row_start = seq_index * row_count
    diag_start = band_index * DIAG
    span_rows = row_count + DIAG
    following = passed_along(right_side, "seq", -1)
    window = jnp.concatenate([right_side, following], axis=0)
    block_reach = band_index * DIAG // row_count
    most_reach = (lax.axis_size("band") - 1) * DIAG // row_count

    def advance(turn_index, carry):
        current, chosen = carry
        current = passed_along(current, "seq", -1)
        chosen = jnp.where(block_reach == turn_index + 1, current, chosen)
        return (current, chosen)

    window = lax.fori_loop(0, most_reach, advance, (window, window))[1]
    first_row = band_index * DIAG % row_count
    window_rows = lax.dynamic_slice_in_dim(window, first_row, span_rows, 0)
    repeated = jnp.tile(window_rows, (row_count + 1, 1))[: row_count * (span_rows + 1)]
    hankel_rows = repeated.reshape(row_count, span_rows + 1, window_rows.shape[1])[:, :DIAG]
    pair_field = (
        left_side[:, None, :].astype(jnp.float32)
        * hankel_rows.astype(jnp.float32)
        * valid_cells(row_start, diag_start, row_count, DIAG, length, band_width)
    ).astype(jnp.bfloat16)
    tile_valid = valid_cells(row_start, diag_start, row_count, DIAG, length, band_width)
    for layer_index in range(CONVS):
        spread = 2**layer_index
        activated = jax.nn.gelu(rms_scale(pair_field, conv_gain[layer_index])).astype(jnp.bfloat16)
        padded = extended(activated, (("seq", 0), ("band", 1)), 2 * spread)
        padded = padded[spread : padded.shape[0] - spread]
        conv_term = shear_conv(padded, conv_kernel[layer_index], spread)
        pair_field = (
            (pair_field.astype(jnp.float32) + conv_term + conv_bias[layer_index]) * tile_valid
        ).astype(jnp.bfloat16)
    contacts = jnp.sum(pair_field.astype(jnp.float32) * contact_weight, axis=-1)
    return (trunk_out, contacts)


def solution(mesh):
    return jax.shard_map(
        local,
        mesh=mesh,
        in_specs=(
            P("seq", "band"),
            P("seq"),
            P(),
            P(None, "band"),
            P(None, "band"),
            P(None, "band"),
            P("band", None),
            P(),
            P(),
            P(),
            P(),
            P(),
            P(),
        ),
        out_specs=(P("seq", "band"), P("seq", "band")),
        check_vma=False,
    )
```

profile of v0, /device:TPU:2, one launch (start us, length us, event | category | flops | bytes accessed | tf_op | source)
XLA Modules:
  0.0 438.1 jit_solution(7441531402315791843)
XLA Ops:
  7.2 32.2 %all_gather.12 = bf16[128,1024]{1,0:T(8,128)(2,1)S(1)} all-gather(bf16[128,128]{1,0:T(8,128)(2,1)} %param.13), channel_id=1, replica_groups=mesh['seq'=32,'band'=8] {'band'}, dimensions={1}, use_global_device_ids=true | all-gather | bytes 294912 | tf_op jit(solution)/shard_map/all_gather | solution.py:87
  41.5 1.9 convolution_convert_fusion.3
  44.1 35.9 %all-gather = bf16[32,1,128]{2,1,0:T(2,128)(2,1)S(1)} all-gather(bf16[1,1,128]{2,1,0:T(2,128)(2,1)S(1)} %convert_bitcast_fusion), channel_id=1, replica_groups=mesh['seq'=32,'band'=8] {'seq'}, dimensions={0}, use_global_device_ids=true | all-gather | bytes 8448 | tf_op jit(solution)/shard_map/all_gather | solution.py:99
  80.1 25.7 %all-gather.4.cloned.1.call-done = bf16[4096,128]{1,0:T(8,128)(2,1)} async-done(((bf16[128,128]{1,0:T(8,128)(2,1)}), bf16[4096,128]{1,0:T(8,128)(2,1)}) %all-gather.4.cloned.1.call-update) | async-done | bytes 1048592 | tf_op jit(solution)/shard_map/all_gather | solution.py:97
  105.8 2.0 fusion.60
  108.3 63.3 %all-gather.6.cloned.1.call-done = bf16[4096,128]{1,0:T(8,128)(2,1)} async-done(((bf16[128,128]{1,0:T(8,128)(2,1)}), bf16[4096,128]{1,0:T(8,128)(2,1)}) %all-gather.6.cloned.1.call-update) | async-done | bytes 1048592 | tf_op jit(solution)/shard_map/all_gather | solution.py:98
  171.6 2.0 convolution_convert_fusion
  174.6 75.3 %reduce-scatter.4.cloned.1.call-done = bf16[128,128]{1,0:T(8,128)(2,1)} async-done(((bf16[1024,128]{1,0:T(8,128)(2,1)}), bf16[128,128]{1,0:T(8,128)(2,1)}) %reduce-scatter.4.cloned.1.call-update) | async-done | bytes 32784
  253.8 87.3 %all-reduce.3.cloned.1.call-done = (bf16[128,128]{1,0:T(8,128)(2,1)}, bf16[128,128]{1,0:T(8,128)(2,1)}) async-done(((bf16[128,128]{1,0:T(8,128)(2,1)}, bf16[128,128]{1,0:T(8,128)(2,1)}), (bf16[128,128]{1,0:T(8,128)(2,1)}, bf16[128,128]{1,0:T(8,128)(2,1)})) %all-reduce.3.cloned.1.call-update) | async-done | bytes 65552 | tf_op jit(solution)/shard_map/psum | solution.py:138
  342.0 1.9 collective-permute-start
  345.5 5.7 %collective-permute-start.1 = (bf16[256,128]{1,0:T(8,128)(2,1)S(1)}, bf16[256,128]{1,0:T(8,128)(2,1)S(1)}, u32[]{:S(2)}, u32[]{:S(2)}) collective-permute-start(bf16[256,128]{1,0:T(8,128)(2,1)S(1)} %pad_maximum_fusion.9), channel_id=1, source_target_pairs={{8,0},{16,8},{24,16},{32,24},{40,32},{48,40},{56,48},{64,56},{72,6... | collective-permute-start | bytes 196616 | tf_op jit(solution)/shard_map/while/body/eval_jaxpr/ppermute | solution.py:15
  354.0 2.7 slice.172
  356.7 7.7 %reshape.195 = bf16[128,161,128]{2,1,0:T(8,128)(2,1)} reshape(bf16[20608,128]{1,0:T(8,128)(2,1)} %slice.172) | data formatting | bytes 10551296 | tf_op jit(solution)/shard_map/reshape | solution.py:163
  369.2 1.9 collective-permute-start.2
  371.1 5.8 %collective-permute-start.3 = (bf16[2,32,128]{2,0,1:T(2,128)(2,1)S(1)}, bf16[2,32,128]{2,0,1:T(2,128)(2,1)S(1)}, u32[]{:S(2)}, u32[]{:S(2)}) collective-permute-start(bf16[2,32,128]{2,0,1:T(2,128)(2,1)S(1)} %get-tuple-element.29), channel_id=1, source_target_pairs={{8,0},{16,8},{24,16},{32,24},{40,32},{48,40},{56,48},{64,56},{72,6... | collective-permute-start | bytes 49160 | tf_op jit(solution)/shard_map/ppermute | solution.py:26
  378.4 1.9 collective-permute-start.5
  382.2 5.8 %collective-permute-done.4 = bf16[132,2,128]{2,0,1:T(8,128)(2,1)S(1)} collective-permute-done((bf16[132,2,128]{2,0,1:T(8,128)(2,1)S(1)}, bf16[132,2,128]{2,0,1:T(8,128)(2,1)S(1)}, u32[]{:S(2)}, u32[]{:S(2)}) %collective-permute-start.4) | collective-permute-done | bytes 67616 | tf_op jit(solution)/shard_map/ppermute | solution.py:26
  390.0 1.9 constant_dynamic-update-slice_fusion
  394.1 3.6 fusion.14
  398.8 1.9 collective-permute-start.6
  400.8 5.8 %collective-permute-start.7 = (bf16[4,32,128]{2,0,1:T(4,128)(2,1)S(1)}, bf16[4,32,128]{2,0,1:T(4,128)(2,1)S(1)}, u32[]{:S(2)}, u32[]{:S(2)}) collective-permute-start(bf16[4,32,128]{2,0,1:T(4,128)(2,1)S(1)} %get-tuple-element.27), channel_id=1, source_target_pairs={{8,0},{16,8},{24,16},{32,24},{40,32},{48,40},{56,48},{64,56},{72,6... | collective-permute-start | bytes 98312 | tf_op jit(solution)/shard_map/ppermute | solution.py:26
  408.2 5.8 %collective-permute-start.9 = (bf16[136,4,128]{2,0,1:T(8,128)(2,1)S(1)}, bf16[136,4,128]{2,0,1:T(8,128)(2,1)S(1)}, u32[]{:S(2)}, u32[]{:S(2)}) collective-permute-start(bf16[136,4,128]{2,0,1:T(8,128)(2,1)S(1)} %get-tuple-element.21), channel_id=1, source_target_pairs={{0,1},{1,2},{2,3},{3,4},{4,5},{5,6},{6,7},{8,9},{9,10},{10,11},{11... | collective-permute-start | bytes 417800 | tf_op jit(solution)/shard_map/ppermute | solution.py:25
  416.6 5.9 %collective-permute-done.8 = bf16[136,4,128]{2,0,1:T(8,128)(2,1)S(1)} collective-permute-done((bf16[136,4,128]{2,0,1:T(8,128)(2,1)S(1)}, bf16[136,4,128]{2,0,1:T(8,128)(2,1)S(1)}, u32[]{:S(2)}, u32[]{:S(2)}) %collective-permute-start.8) | collective-permute-done | bytes 139296 | tf_op jit(solution)/shard_map/ppermute | solution.py:26
  428.0 3.5 multiply_reduce_fusion
  (90 shorter events, 36.3 us)
Async XLA Ops:
  7.2 98.6 %copy-start = (bf16[1024,128]{1,0:T(8,128)(2,1)S(1)}, bf16[1024,128]{1,0:T(8,128)(2,1)}, u32[]{:S(2)}) copy-start(bf16[1024,128]{1,0:T(8,128)(2,1)} %param.16) | copy-start | bytes 786436
  7.2 98.6 %all-gather.4.cloned.1.call-start = ((), (), s32[]{:S(2)}) async-start(), calls=%async_computation.1 | async-start | bytes 1081344 | tf_op jit(solution)/shard_map/all_gather | solution.py:97
  41.5 130.1 %all-gather.6.cloned.1.call-start = ((), (), s32[]{:S(2)}) async-start(), calls=%async_computation.2 | async-start | bytes 1081344 | tf_op jit(solution)/shard_map/all_gather | solution.py:98
  43.4 206.4 %reduce-scatter.4.cloned.1.call-start = ((), (), s32[]{:S(2)}) async-start(), calls=%async_computation.3 | async-start | bytes 294912
  105.8 65.8 %copy-start.3 = (bf16[128,1024]{1,0:T(8,128)(2,1)S(1)}, bf16[128,1024]{1,0:T(8,128)(2,1)}, u32[]{:S(2)}) copy-start(bf16[128,1024]{1,0:T(8,128)(2,1)} %param.19) | copy-start | bytes 786436
  171.6 2.9 copy-start.7
  171.6 3.0 copy-start.1
  171.6 79.2 %copy-start.4 = (bf16[128,128]{1,0:T(8,128)(2,1)S(1)}, bf16[128,128]{1,0:T(8,128)(2,1)}, u32[]{:S(2)}) copy-start(bf16[128,128]{1,0:T(8,128)(2,1)} %param.13) | copy-start | bytes 98308
  173.5 177.7 %copy-start.5 = (f32[2,128]{1,0:T(2,128)S(1)}, f32[2,128]{1,0:T(2,128)}, u32[]{:S(2)}) copy-start(f32[2,128]{1,0:T(2,128)} %param.22) | copy-start | bytes 3076
  174.4 166.7 %all-reduce.3.cloned.1.call-start = ((), (), s32[]{:S(2)}) async-start(), calls=%async_computation.4 | async-start | bytes 131072 | tf_op jit(solution)/shard_map/psum | solution.py:138
  250.8 103.2 %copy-start.2 = (bf16[128,128]{1,0:T(8,128)(2,1)}, bf16[128,128]{1,0:T(8,128)(2,1)S(1)}, u32[]{:S(2)}) copy-start(bf16[128,128]{1,0:T(8,128)(2,1)S(1)} %add_convert_fusion) | copy-start | bytes 98308
  342.0 3.5 collective-permute-start
  345.5 7.6 %collective-permute-start.1 = (bf16[256,128]{1,0:T(8,128)(2,1)S(1)}, bf16[256,128]{1,0:T(8,128)(2,1)S(1)}, u32[]{:S(2)}, u32[]{:S(2)}) collective-permute-start(bf16[256,128]{1,0:T(8,128)(2,1)S(1)} %pad_maximum_fusion.9), channel_id=1, source_target_pairs={{8,0},{16,8},{24,16},{32,24},{40,32},{48,40},{56,48},{64,56},{72,6... | collective-permute-start | bytes 196616 | tf_op jit(solution)/shard_map/while/body/eval_jaxpr/ppermute | solution.py:15
  365.7 11.2 %copy-start.6 = (f32[2,128]{1,0:T(2,128)S(1)}, f32[2,128]{1,0:T(2,128)}, u32[]{:S(2)}) copy-start(f32[2,128]{1,0:T(2,128)} %param.24) | copy-start | bytes 3076
  369.2 7.8 %collective-permute-start.2 = (bf16[2,32,128]{2,0,1:T(2,128)(2,1)S(1)}, bf16[2,32,128]{2,0,1:T(2,128)(2,1)S(1)}, u32[]{:S(2)}, u32[]{:S(2)}) collective-permute-start(bf16[2,32,128]{2,0,1:T(2,128)(2,1)S(1)} %get-tuple-element.30), channel_id=1, source_target_pairs={{0,8},{8,16},{16,24},{24,32},{32,40},{40,48},{48,56},{56,64},{64,7... | collective-permute-start | bytes 49160 | tf_op jit(solution)/shard_map/ppermute | solution.py:25
  371.1 7.2 %collective-permute-start.3 = (bf16[2,32,128]{2,0,1:T(2,128)(2,1)S(1)}, bf16[2,32,128]{2,0,1:T(2,128)(2,1)S(1)}, u32[]{:S(2)}, u32[]{:S(2)}) collective-permute-start(bf16[2,32,128]{2,0,1:T(2,128)(2,1)S(1)} %get-tuple-element.29), channel_id=1, source_target_pairs={{8,0},{16,8},{24,16},{32,24},{40,32},{48,40},{56,48},{64,56},{72,6... | collective-permute-start | bytes 49160 | tf_op jit(solution)/shard_map/ppermute | solution.py:26
  378.4 3.9 collective-permute-start.5
  380.3 7.7 %collective-permute-start.4 = (bf16[132,2,128]{2,0,1:T(8,128)(2,1)S(1)}, bf16[132,2,128]{2,0,1:T(8,128)(2,1)S(1)}, u32[]{:S(2)}, u32[]{:S(2)}) collective-permute-start(bf16[132,2,128]{2,0,1:T(8,128)(2,1)S(1)} %get-tuple-element.26), channel_id=1, source_target_pairs={{1,0},{2,1},{3,2},{4,3},{5,4},{6,5},{7,6},{9,8},{10,9},{11,10},{12... | collective-permute-start | bytes 202760 | tf_op jit(solution)/shard_map/ppermute | solution.py:26
  398.8 7.7 %collective-permute-start.6 = (bf16[4,32,128]{2,0,1:T(4,128)(2,1)S(1)}, bf16[4,32,128]{2,0,1:T(4,128)(2,1)S(1)}, u32[]{:S(2)}, u32[]{:S(2)}) collective-permute-start(bf16[4,32,128]{2,0,1:T(4,128)(2,1)S(1)} %get-tuple-element.28), channel_id=1, source_target_pairs={{0,8},{8,16},{16,24},{24,32},{32,40},{40,48},{48,56},{56,64},{64,7... | collective-permute-start | bytes 98312 | tf_op jit(solution)/shard_map/ppermute | solution.py:25
  400.8 7.3 %collective-permute-start.7 = (bf16[4,32,128]{2,0,1:T(4,128)(2,1)S(1)}, bf16[4,32,128]{2,0,1:T(4,128)(2,1)S(1)}, u32[]{:S(2)}, u32[]{:S(2)}) collective-permute-start(bf16[4,32,128]{2,0,1:T(4,128)(2,1)S(1)} %get-tuple-element.27), channel_id=1, source_target_pairs={{8,0},{16,8},{24,16},{32,24},{40,32},{48,40},{56,48},{64,56},{72,6... | collective-permute-start | bytes 98312 | tf_op jit(solution)/shard_map/ppermute | solution.py:26
  408.2 8.4 %collective-permute-start.9 = (bf16[136,4,128]{2,0,1:T(8,128)(2,1)S(1)}, bf16[136,4,128]{2,0,1:T(8,128)(2,1)S(1)}, u32[]{:S(2)}, u32[]{:S(2)}) collective-permute-start(bf16[136,4,128]{2,0,1:T(8,128)(2,1)S(1)} %get-tuple-element.21), channel_id=1, source_target_pairs={{0,1},{1,2},{2,3},{3,4},{4,5},{5,6},{6,7},{8,9},{9,10},{10,11},{11... | collective-permute-start | bytes 417800 | tf_op jit(solution)/shard_map/ppermute | solution.py:25
  414.0 8.5 %collective-permute-start.8 = (bf16[136,4,128]{2,0,1:T(8,128)(2,1)S(1)}, bf16[136,4,128]{2,0,1:T(8,128)(2,1)S(1)}, u32[]{:S(2)}, u32[]{:S(2)}) collective-permute-start(bf16[136,4,128]{2,0,1:T(8,128)(2,1)S(1)} %get-tuple-element.22), channel_id=1, source_target_pairs={{1,0},{2,1},{3,2},{4,3},{5,4},{6,5},{7,6},{9,8},{10,9},{11,10},{12... | collective-permute-start | bytes 417800 | tf_op jit(solution)/shard_map/ppermute | solution.py:26
  426.8 1.2 copy-start.8
Sparse Core Ops, SparseCore 0:
  41.6 64.1 all-gather.3
  108.2 63.2 all-gather.5
  175.4 74.4 reduce-scatter.3
  253.9 87.1 all-reduce.2
where the time goes:
time: 439 us; the launch traced here: 438 us
  waiting for transfers between devices  270 us (62%)
  blocking collectives  68.2 us (16%)
  starting transfers between devices  33.9 us (8%)
  local copies, waits for them, and re-layouts  20.2 us (5%)
  matrix products  17.8 us (4%)
  between operations  14.3 us (3%)
  other arithmetic  13.3 us (3%)
    psum x1, waiting for transfers between devices, local(): lax.psum(jnp.dot(trunk_out, rows_right, preferred_element_type=jnp.float3...  87.3 us
    unnamed x5, waiting for transfers between devices  75.3 us
    all_gather x1, waiting for transfers between devices, local(): value_piece = lax.all_gather(value, 'seq', axis=0, tiled=True)  63.3 us
    all_gather x1, blocking collectives, local(): offset_piece = lax.all_gather(key_offset, 'seq', axis=0, tiled=True)  35.9 us
    all_gather x1, blocking collectives, local(): gathered = lax.all_gather(tokens, 'band', axis=1, tiled=True)  32.2 us
    all_gather x1, waiting for transfers between devices, local(): key_piece = lax.all_gather(key_rows, 'seq', axis=0, tiled=True)  25.7 us
    ppermute x4, waiting for transfers between devices, extended(): after = lax.ppermute(initial, axis, down)  14.6 us
    ppermute x4, starting transfers between devices, extended(): after = lax.ppermute(initial, axis, down)  14.5 us
  transfers between devices with their start and end apart: 14, of which 12 were waited for; matrix products, arithmetic and copies ran while one was open for 1% of the time, Pallas kernels for 0%

commit v1 on v0

--- a/solution.py
+++ b/solution.py
@@ -135,9 +135,14 @@
             jnp.dot(trunk_out, rows_left, preferred_element_type=jnp.float32).astype(jnp.bfloat16),
             "band",
         ).astype(jnp.float32),
-        lax.psum(
-            jnp.dot(trunk_out, rows_right, preferred_element_type=jnp.float32).astype(jnp.bfloat16),
-            "band",
+        jnp.sum(
+            lax.all_gather(
+                jnp.dot(trunk_out, rows_right, preferred_element_type=jnp.float32).astype(
+                    jnp.bfloat16
+                ),
+                "band",
+            ),
+            axis=0,
         ).astype(jnp.float32),
     )
     left_side = part_left.astype(jnp.bfloat16) * keep_rows

time: 439 us -> 423 us (0.964)
  waiting for transfers between devices: 270 us -> 183 us
  blocking collectives: 68.2 us -> 143 us
    psum x1 -> x0, waiting for transfers between devices: 87.3 us -> none  [local(): lax.psum(jnp.dot(trunk_out, rows_right, preferred_element_type=jnp.float3...]
    psum x0 -> x1, blocking collectives: none -> 39.7 us  [local(): lax.psum(jnp.dot(trunk_out, rows_left, preferred_element_type=jnp.float32...]
    all_gather x0 -> x1, blocking collectives: none -> 34.7 us  [local(): lax.all_gather(jnp.dot(trunk_out, rows_right, preferred_element_type=jnp....]
    unnamed x5 -> x4, waiting for transfers between devices: 75.3 us -> 75.4 us
  transfers between devices with their start and end apart: 14 -> 13, of which waited for: 12 -> 11; matrix products, arithmetic and copies ran while one was open for 1% -> 1% of each run, Pallas kernels for 0% -> 0%
where the time goes in v1:
time: 423 us; the launch traced here: 422 us
  waiting for transfers between devices  183 us (43%)
  blocking collectives  143 us (34%)
  starting transfers between devices  33.2 us (8%)
  local copies, waits for them, and re-layouts  20.3 us (5%)
  matrix products  16.6 us (4%)
  between operations  14.3 us (3%)
  other arithmetic  12.6 us (3%)
    unnamed x4, waiting for transfers between devices  75.4 us
    all_gather x1, waiting for transfers between devices, local(): value_piece = lax.all_gather(value, 'seq', axis=0, tiled=True)  63.3 us
    psum x1, blocking collectives, local(): lax.psum(jnp.dot(trunk_out, rows_left, preferred_element_type=jnp.float32...  39.7 us
    all_gather x1, blocking collectives, local(): offset_piece = lax.all_gather(key_offset, 'seq', axis=0, tiled=True)  35.9 us
    all_gather x1, blocking collectives, local(): lax.all_gather(jnp.dot(trunk_out, rows_right, preferred_element_type=jnp....  34.7 us
    all_gather x1, blocking collectives, local(): gathered = lax.all_gather(tokens, 'band', axis=1, tiled=True)  32.2 us
    all_gather x1, waiting for transfers between devices, local(): key_piece = lax.all_gather(key_rows, 'seq', axis=0, tiled=True)  25.7 us
    ppermute x4, waiting for transfers between devices, extended(): after = lax.ppermute(initial, axis, down)  14.6 us
  transfers between devices with their start and end apart: 13, of which 11 were waited for; matrix products, arithmetic and copies ran while one was open for 1% of the time, Pallas kernels for 0%

profile of v1, /device:TPU:2, one launch (start us, length us, event | category | flops | bytes accessed | tf_op | source)
XLA Modules:
  0.0 422.4 jit_solution(5975733706799160766)
XLA Ops:
  7.2 32.2 %all_gather.18 = bf16[128,1024]{1,0:T(8,128)(2,1)S(1)} all-gather(bf16[128,128]{1,0:T(8,128)(2,1)} %param.13), channel_id=1, replica_groups=mesh['seq'=32,'band'=8] {'band'}, dimensions={1}, use_global_device_ids=true | all-gather | bytes 294912 | tf_op jit(solution)/shard_map/all_gather | solution.py:87
  41.5 1.9 convolution_convert_fusion.3
  44.1 35.9 %all-gather.1 = bf16[32,1,128]{2,1,0:T(2,128)(2,1)S(1)} all-gather(bf16[1,1,128]{2,1,0:T(2,128)(2,1)S(1)} %convert_bitcast_fusion), channel_id=1, replica_groups=mesh['seq'=32,'band'=8] {'seq'}, dimensions={0}, use_global_device_ids=true | all-gather | bytes 8448 | tf_op jit(solution)/shard_map/all_gather | solution.py:99
  80.1 25.7 %all-gather.5.cloned.1.call-done = bf16[4096,128]{1,0:T(8,128)(2,1)} async-done(((bf16[128,128]{1,0:T(8,128)(2,1)}), bf16[4096,128]{1,0:T(8,128)(2,1)}) %all-gather.5.cloned.1.call-update) | async-done | bytes 1048592 | tf_op jit(solution)/shard_map/all_gather | solution.py:97
  105.8 2.0 fusion.60
  108.3 63.3 %all-gather.7.cloned.1.call-done = bf16[4096,128]{1,0:T(8,128)(2,1)} async-done(((bf16[128,128]{1,0:T(8,128)(2,1)}), bf16[4096,128]{1,0:T(8,128)(2,1)}) %all-gather.7.cloned.1.call-update) | async-done | bytes 1048592 | tf_op jit(solution)/shard_map/all_gather | solution.py:98
  171.6 2.0 convolution_convert_fusion
  174.5 75.3 %reduce-scatter.4.cloned.1.call-done = bf16[128,128]{1,0:T(8,128)(2,1)} async-done(((bf16[1024,128]{1,0:T(8,128)(2,1)}), bf16[128,128]{1,0:T(8,128)(2,1)}) %reduce-scatter.4.cloned.1.call-update) | async-done | bytes 32784
  251.7 39.7 %psum.7 = bf16[128,128]{1,0:T(8,128)(2,1)S(1)} all-reduce(bf16[128,128]{1,0:T(8,128)(2,1)S(1)} %convolution_convert_fusion.2), channel_id=1, replica_groups=mesh['seq'=32,'band'=8] {'band'}, use_global_device_ids=true, to_apply=%region_4.0 | all-reduce | flops 16384 | bytes 65536 | tf_op jit(solution)/shard_map/psum | solution.py:134
  292.3 34.7 %all-gather = bf16[1024,128]{1,0:T(8,128)(2,1)S(1)} all-gather(bf16[128,128]{1,0:T(8,128)(2,1)S(1)} %convolution_convert_fusion.1), channel_id=2, replica_groups=mesh['seq'=32,'band'=8] {'band'}, dimensions={0}, use_global_device_ids=true | all-gather | bytes 294912 | tf_op jit(solution)/shard_map/all_gather | solution.py:139
  327.1 1.9 collective-permute-start
  330.6 5.7 %collective-permute-start.1 = (bf16[256,128]{1,0:T(8,128)(2,1)S(1)}, bf16[256,128]{1,0:T(8,128)(2,1)S(1)}, u32[]{:S(2)}, u32[]{:S(2)}) collective-permute-start(bf16[256,128]{1,0:T(8,128)(2,1)S(1)} %pad_maximum_fusion.9), channel_id=1, source_target_pairs={{8,0},{16,8},{24,16},{32,24},{40,32},{48,40},{56,48},{64,56},{72,6... | collective-permute-start | bytes 196616 | tf_op jit(solution)/shard_map/while/body/eval_jaxpr/ppermute | solution.py:15
  339.0 2.7 slice.172
  341.8 7.8 %reshape.195 = bf16[128,161,128]{2,1,0:T(8,128)(2,1)} reshape(bf16[20608,128]{1,0:T(8,128)(2,1)} %slice.172) | data formatting | bytes 10551296 | tf_op jit(solution)/shard_map/reshape | solution.py:168
  354.3 1.9 collective-permute-start.2
  356.2 5.8 %collective-permute-start.3 = (bf16[2,32,128]{2,0,1:T(2,128)(2,1)S(1)}, bf16[2,32,128]{2,0,1:T(2,128)(2,1)S(1)}, u32[]{:S(2)}, u32[]{:S(2)}) collective-permute-start(bf16[2,32,128]{2,0,1:T(2,128)(2,1)S(1)} %get-tuple-element.27), channel_id=1, source_target_pairs={{8,0},{16,8},{24,16},{32,24},{40,32},{48,40},{56,48},{64,56},{72,6... | collective-permute-start | bytes 49160 | tf_op jit(solution)/shard_map/ppermute | solution.py:26
  366.7 5.8 %collective-permute-done.4 = bf16[132,2,128]{2,0,1:T(8,128)(2,1)S(1)} collective-permute-done((bf16[132,2,128]{2,0,1:T(8,128)(2,1)S(1)}, bf16[132,2,128]{2,0,1:T(8,128)(2,1)S(1)}, u32[]{:S(2)}, u32[]{:S(2)}) %collective-permute-start.4) | collective-permute-done | bytes 67616 | tf_op jit(solution)/shard_map/ppermute | solution.py:26
  374.5 1.9 constant_dynamic-update-slice_fusion
  378.6 3.6 fusion.14
  383.3 1.9 collective-permute-start.6
  385.2 5.8 %collective-permute-start.7 = (bf16[4,32,128]{2,0,1:T(4,128)(2,1)S(1)}, bf16[4,32,128]{2,0,1:T(4,128)(2,1)S(1)}, u32[]{:S(2)}, u32[]{:S(2)}) collective-permute-start(bf16[4,32,128]{2,0,1:T(4,128)(2,1)S(1)} %get-tuple-element.25), channel_id=1, source_target_pairs={{8,0},{16,8},{24,16},{32,24},{40,32},{48,40},{56,48},{64,56},{72,6... | collective-permute-start | bytes 98312 | tf_op jit(solution)/shard_map/ppermute | solution.py:26
  392.6 5.7 %collective-permute-start.9 = (bf16[136,4,128]{2,0,1:T(8,128)(2,1)S(1)}, bf16[136,4,128]{2,0,1:T(8,128)(2,1)S(1)}, u32[]{:S(2)}, u32[]{:S(2)}) collective-permute-start(bf16[136,4,128]{2,0,1:T(8,128)(2,1)S(1)} %get-tuple-element.14), channel_id=1, source_target_pairs={{0,1},{1,2},{2,3},{3,4},{4,5},{5,6},{6,7},{8,9},{9,10},{10,11},{11... | collective-permute-start | bytes 417800 | tf_op jit(solution)/shard_map/ppermute | solution.py:25
  400.9 5.9 %collective-permute-done.8 = bf16[136,4,128]{2,0,1:T(8,128)(2,1)S(1)} collective-permute-done((bf16[136,4,128]{2,0,1:T(8,128)(2,1)S(1)}, bf16[136,4,128]{2,0,1:T(8,128)(2,1)S(1)}, u32[]{:S(2)}, u32[]{:S(2)}) %collective-permute-start.8) | collective-permute-done | bytes 139296 | tf_op jit(solution)/shard_map/ppermute | solution.py:26
  412.4 3.5 multiply_reduce_fusion
  (90 shorter events, 35.6 us)
Async XLA Ops:
  7.2 98.6 %copy-start = (bf16[1024,128]{1,0:T(8,128)(2,1)S(1)}, bf16[1024,128]{1,0:T(8,128)(2,1)}, u32[]{:S(2)}) copy-start(bf16[1024,128]{1,0:T(8,128)(2,1)} %param.16) | copy-start | bytes 786436
  7.2 98.6 %all-gather.5.cloned.1.call-start = ((), (), s32[]{:S(2)}) async-start(), calls=%async_computation.1 | async-start | bytes 1081344 | tf_op jit(solution)/shard_map/all_gather | solution.py:97
  41.5 130.1 %all-gather.7.cloned.1.call-start = ((), (), s32[]{:S(2)}) async-start(), calls=%async_computation.2 | async-start | bytes 1081344 | tf_op jit(solution)/shard_map/all_gather | solution.py:98
  43.4 206.4 %reduce-scatter.4.cloned.1.call-start = ((), (), s32[]{:S(2)}) async-start(), calls=%async_computation.3 | async-start | bytes 294912
  105.8 65.8 %copy-start.3 = (bf16[128,1024]{1,0:T(8,128)(2,1)S(1)}, bf16[128,1024]{1,0:T(8,128)(2,1)}, u32[]{:S(2)}) copy-start(bf16[128,1024]{1,0:T(8,128)(2,1)} %param.19) | copy-start | bytes 786436
  171.6 2.9 copy-start.7
  171.6 2.9 copy-start.1
  171.6 79.2 %copy-start.4 = (bf16[128,128]{1,0:T(8,128)(2,1)S(1)}, bf16[128,128]{1,0:T(8,128)(2,1)}, u32[]{:S(2)}) copy-start(bf16[128,128]{1,0:T(8,128)(2,1)} %param.13) | copy-start | bytes 98308
  173.5 162.8 %copy-start.5 = (f32[2,128]{1,0:T(2,128)S(1)}, f32[2,128]{1,0:T(2,128)}, u32[]{:S(2)}) copy-start(f32[2,128]{1,0:T(2,128)} %param.22) | copy-start | bytes 3076
  250.8 88.3 %copy-start.2 = (bf16[128,128]{1,0:T(8,128)(2,1)}, bf16[128,128]{1,0:T(8,128)(2,1)S(1)}, u32[]{:S(2)}) copy-start(bf16[128,128]{1,0:T(8,128)(2,1)S(1)} %add_convert_fusion) | copy-start | bytes 98308
  327.1 3.5 collective-permute-start
  330.6 7.6 %collective-permute-start.1 = (bf16[256,128]{1,0:T(8,128)(2,1)S(1)}, bf16[256,128]{1,0:T(8,128)(2,1)S(1)}, u32[]{:S(2)}, u32[]{:S(2)}) collective-permute-start(bf16[256,128]{1,0:T(8,128)(2,1)S(1)} %pad_maximum_fusion.9), channel_id=1, source_target_pairs={{8,0},{16,8},{24,16},{32,24},{40,32},{48,40},{56,48},{64,56},{72,6... | collective-permute-start | bytes 196616 | tf_op jit(solution)/shard_map/while/body/eval_jaxpr/ppermute | solution.py:15
  350.8 11.2 %copy-start.6 = (f32[2,128]{1,0:T(2,128)S(1)}, f32[2,128]{1,0:T(2,128)}, u32[]{:S(2)}) copy-start(f32[2,128]{1,0:T(2,128)} %param.24) | copy-start | bytes 3076
  354.3 7.8 %collective-permute-start.2 = (bf16[2,32,128]{2,0,1:T(2,128)(2,1)S(1)}, bf16[2,32,128]{2,0,1:T(2,128)(2,1)S(1)}, u32[]{:S(2)}, u32[]{:S(2)}) collective-permute-start(bf16[2,32,128]{2,0,1:T(2,128)(2,1)S(1)} %get-tuple-element.28), channel_id=1, source_target_pairs={{0,8},{8,16},{16,24},{24,32},{32,40},{40,48},{48,56},{56,64},{64,7... | collective-permute-start | bytes 49160 | tf_op jit(solution)/shard_map/ppermute | solution.py:25
  356.2 7.2 %collective-permute-start.3 = (bf16[2,32,128]{2,0,1:T(2,128)(2,1)S(1)}, bf16[2,32,128]{2,0,1:T(2,128)(2,1)S(1)}, u32[]{:S(2)}, u32[]{:S(2)}) collective-permute-start(bf16[2,32,128]{2,0,1:T(2,128)(2,1)S(1)} %get-tuple-element.27), channel_id=1, source_target_pairs={{8,0},{16,8},{24,16},{32,24},{40,32},{48,40},{56,48},{64,56},{72,6... | collective-permute-start | bytes 49160 | tf_op jit(solution)/shard_map/ppermute | solution.py:26
  363.5 3.2 collective-permute-start.5
  364.8 7.7 %collective-permute-start.4 = (bf16[132,2,128]{2,0,1:T(8,128)(2,1)S(1)}, bf16[132,2,128]{2,0,1:T(8,128)(2,1)S(1)}, u32[]{:S(2)}, u32[]{:S(2)}) collective-permute-start(bf16[132,2,128]{2,0,1:T(8,128)(2,1)S(1)} %get-tuple-element.24), channel_id=1, source_target_pairs={{1,0},{2,1},{3,2},{4,3},{5,4},{6,5},{7,6},{9,8},{10,9},{11,10},{12... | collective-permute-start | bytes 202760 | tf_op jit(solution)/shard_map/ppermute | solution.py:26
  383.3 7.7 %collective-permute-start.6 = (bf16[4,32,128]{2,0,1:T(4,128)(2,1)S(1)}, bf16[4,32,128]{2,0,1:T(4,128)(2,1)S(1)}, u32[]{:S(2)}, u32[]{:S(2)}) collective-permute-start(bf16[4,32,128]{2,0,1:T(4,128)(2,1)S(1)} %get-tuple-element.26), channel_id=1, source_target_pairs={{0,8},{8,16},{16,24},{24,32},{32,40},{40,48},{48,56},{56,64},{64,7... | collective-permute-start | bytes 98312 | tf_op jit(solution)/shard_map/ppermute | solution.py:25
  385.2 7.3 %collective-permute-start.7 = (bf16[4,32,128]{2,0,1:T(4,128)(2,1)S(1)}, bf16[4,32,128]{2,0,1:T(4,128)(2,1)S(1)}, u32[]{:S(2)}, u32[]{:S(2)}) collective-permute-start(bf16[4,32,128]{2,0,1:T(4,128)(2,1)S(1)} %get-tuple-element.25), channel_id=1, source_target_pairs={{8,0},{16,8},{24,16},{32,24},{40,32},{48,40},{56,48},{64,56},{72,6... | collective-permute-start | bytes 98312 | tf_op jit(solution)/shard_map/ppermute | solution.py:26
  392.6 8.3 %collective-permute-start.9 = (bf16[136,4,128]{2,0,1:T(8,128)(2,1)S(1)}, bf16[136,4,128]{2,0,1:T(8,128)(2,1)S(1)}, u32[]{:S(2)}, u32[]{:S(2)}) collective-permute-start(bf16[136,4,128]{2,0,1:T(8,128)(2,1)S(1)} %get-tuple-element.14), channel_id=1, source_target_pairs={{0,1},{1,2},{2,3},{3,4},{4,5},{5,6},{6,7},{8,9},{9,10},{10,11},{11... | collective-permute-start | bytes 417800 | tf_op jit(solution)/shard_map/ppermute | solution.py:25
  398.4 8.5 %collective-permute-start.8 = (bf16[136,4,128]{2,0,1:T(8,128)(2,1)S(1)}, bf16[136,4,128]{2,0,1:T(8,128)(2,1)S(1)}, u32[]{:S(2)}, u32[]{:S(2)}) collective-permute-start(bf16[136,4,128]{2,0,1:T(8,128)(2,1)S(1)} %get-tuple-element.20), channel_id=1, source_target_pairs={{1,0},{2,1},{3,2},{4,3},{5,4},{6,5},{7,6},{9,8},{10,9},{11,10},{12... | collective-permute-start | bytes 417800 | tf_op jit(solution)/shard_map/ppermute | solution.py:26
  411.2 1.2 copy-start.8
Sparse Core Ops, SparseCore 0:
  41.6 64.1 all-gather.4
  108.2 63.2 all-gather.6
  175.4 74.4 reduce-scatter.3
